TPU v7x, 32 devices: a whole 2x2x4 slice. The times are simulated.
32 devices in a mesh: dom: 8 (over y, x, core), rep: 4 (over z).
Axes of the slice: x: 2, y: 2, z: 4, core: 2. Of those that a mesh axis runs over, the one named last changes fastest.
Arguments:
- features: float32 [2048, 256], P('dom'), may hold values from -6 to 6
- tile_values: bfloat16 [8, 64, 128, 128], P('dom', 'rep'), may hold values from 0 to 0.03125
- tile_rows: int32 [8, 64], P('dom', 'rep'), may hold values from 0 to 1
- tile_cols: int32 [8, 64], P('dom', 'rep'), may hold values from 0 to 15, as said below
- weight: float32 [256, 256], replicated, may hold values from -0.375 to 0.375
- bias: float32 [256], replicated, may hold values from -3 to 3
- cotangent: float32 [2048, 256], P('dom'), may hold values from -6 to 6
Outputs:
- activations: float32 [2048, 256], P('dom')
- grad_features: float32 [2048, 256], P('dom')
- grad_weight: float32 [256, 256], replicated
- grad_bias: float32 [256], replicated
Inputs may be any that keep to these rules, and one draw needn't show every extreme that they name: `tile_cols`: within each share of 16 consecutive tiles of a partition, every tile column 0 to 15 appears exactly once.
All inputs are finite; a program needn't handle non-finite values.
Results may differ from a plain program's by a relative error of at most 0.0003.
Values sent between devices are 32-bit elements; how exact they have to be, the bound alone decides.
A program may use at most 64 MiB of HBM per device.

v0:
```python
import jax
import jax.numpy as jnp
from jax import lax
from jax.sharding import PartitionSpec as P


def body(features, tile_values, tile_rows, tile_cols, weight, bias, cotangent):
    highest = lax.Precision.HIGHEST
    values = tile_values[0].astype(jnp.float32)
    row_ids = tile_rows[0]
    col_ids = tile_cols[0]
    tile_size = values.shape[1]
    node_rows = features.shape[0]
    feat_width = features.shape[1]
    row_blocks = node_rows // tile_size
    shard_piece = lax.all_gather(features, "dom", axis=0, tiled=True)
    block_count = shard_piece.shape[0] // tile_size
    blocks = shard_piece.reshape(block_count, tile_size, feat_width)
    offsets = col_ids[:, None]
    select = (offsets == jnp.arange(block_count, dtype=jnp.int32)[None, :]).astype(jnp.float32)
    selected = jnp.einsum("sn,nif->sif", select, blocks, precision=highest)
    products = jnp.einsum("sij,sjf->sif", values, selected, precision=highest)
    row_select = (row_ids[None, :] == jnp.arange(row_blocks, dtype=jnp.int32)[:, None]).astype(
        jnp.float32
    )
    partial_rows = jnp.einsum("bs,sif->bif", row_select, products, precision=highest).reshape(
        node_rows, feat_width
    )
    aggregated = lax.psum(partial_rows, "rep")
    before = jnp.dot(aggregated, weight, precision=highest) + bias
    gate_value = jax.nn.sigmoid(before)
    output = before * gate_value
    grad_pre = cotangent * gate_value * (1.0 + before * (1.0 - gate_value))
    messages = jnp.dot(grad_pre, weight.T, precision=highest)
    weight_term = jnp.dot(aggregated.T, grad_pre, precision=highest)
    activations, messages, weight_term, bias_term = (
        output,
        messages,
        weight_term,
        jnp.sum(grad_pre, axis=0),
    )
    grad_weight, grad_bias = lax.psum((weight_term, bias_term), "dom")
    message_blocks = messages.reshape(row_blocks, tile_size, feat_width)
    picked_messages = jnp.einsum("bs,bif->sif", row_select, message_blocks, precision=highest)
    returned = jnp.einsum("sji,sjf->sif", values, picked_messages, precision=highest)
    block_count = node_rows * lax.axis_size("dom") // tile_size
    offsets = col_ids[None, :]
    select = (offsets == jnp.arange(block_count, dtype=jnp.int32)[:, None]).astype(jnp.float32)
    source_part = lax.psum_scatter(
        jnp.einsum("ns,sif->nif", select, returned, precision=highest).reshape(
            node_rows * lax.axis_size("dom"), feat_width
        ),
        "dom",
        scatter_dimension=0,
        tiled=True,
    )
    grad_features = lax.psum(source_part, "rep")
    return (activations, grad_features, grad_weight, grad_bias)


def solution(mesh):
    return jax.shard_map(
        body,
        mesh=mesh,
        in_specs=(
            P("dom", None),
            P("dom", "rep", None, None),
            P("dom", "rep"),
            P("dom", "rep"),
            P(),
            P(),
            P("dom", None),
        ),
        out_specs=(P("dom", None), P("dom", None), P(), P()),
        check_vma=False,
    )
```

profile of v0, /device:TPU:0, one launch (start us, length us, event | category | flops | bytes accessed | tf_op | source)
XLA Modules:
  0.0 246.7 jit_solution(1948898299063535947)
XLA Ops:
  7.2 0.0 copy-start
  7.2 0.0 all-gather.2.cloned.1.call-start
  7.2 0.7 all-gather.2.cloned.1.call-update
  7.9 0.0 all-reduce.4.cloned.1.call-start
  8.0 32.6 %all-gather.2.cloned.1.call-done = f32[2048,256]{1,0:T(8,128)} async-done(((f32[256,256]{1,0:T(8,128)}), f32[2048,256]{1,0:T(8,128)}) %all-gather.2.cloned.1.call-update) | async-done | bytes 2097168 | tf_op jit(solution)/shard_map/all_gather | solution.py:16
  40.5 3.9 %fusion.8 = f32[16,128,256]{2,0,1:T(8,128)S(1)} fusion(f32[16,128,256]{2,1,0:T(8,128)} %bitcast.35, s32[16]{0:T(128)} %bitcast.40), kind=kOutput, calls=%fused_computation.8 | convolution fusion | flops 100663552 | bytes 4194368 | tf_op jit(solution)/shard_map/sn,nif->sif/dot_general | solution.py:21
  44.5 0.0 copy-done
  44.5 4.1 %fusion.6 = f32[16,256,128]{2,1,0:T(8,128)} fusion(f32[16,128,256]{2,0,1:T(8,128)S(1)} %fusion.8, bf16[1,16,128,128]{3,2,1,0:T(8,128)(2,1)S(1)} %copy-done), kind=kOutput, calls=%fused_computation.6 | convolution fusion | flops 805306368 | bytes 4718592 | tf_op jit(solution)/shard_map/sij,sjf->sif/dot_general | solution.py:22
  48.5 0.0 copy-start.3
  48.5 2.2 copy.15
  50.8 0.0 copy-start.1
  50.8 0.0 copy-start.5
  50.8 0.0 copy-start.6
  50.8 0.0 copy-done.3
  50.8 0.8 fusion.2
  51.6 0.7 copy.11
  52.4 0.0 all-reduce.4.cloned.1.call-update
  52.4 0.2 reduce-scatter.2.cloned.1.call-start
  52.6 35.2 %all-reduce.4.cloned.1.call-done = f32[256,256]{1,0:T(8,128)} async-done(((f32[256,256]{1,0:T(8,128)}), f32[256,256]{1,0:T(8,128)}) %all-reduce.4.cloned.1.call-update) | async-done | bytes 262160 | tf_op jit(solution)/shard_map/psum | solution.py:29
  87.9 0.0 copy-done.1
  87.9 0.0 copy-done.5
  87.9 0.0 copy-done.6
  87.9 2.1 fusion.25
  90.0 0.4 fusion.26
  90.4 1.1 fusion.12
  91.5 2.7 %fusion.4 = f32[16,256,128]{2,1,0:T(8,128)S(1)} fusion(f32[16,128,256]{2,0,1:T(8,128)S(1)} %fusion.12, bf16[1,16,128,128]{3,2,1,0:T(8,128)(2,1)S(1)} %copy-done), kind=kOutput, calls=%fused_computation.4 | convolution fusion | flops 805306368 | bytes 4718592 | tf_op jit(solution)/shard_map/sji,sjf->sif/dot_general | solution.py:45
  94.3 0.0 copy-start.4
  94.3 2.1 copy.18
  96.4 0.0 copy-done.4
  96.4 2.7 %fusion = f32[16,128,256]{2,0,1:T(8,128)S(1)} fusion(f32[16,256,128]{1,0,2:T(8,128)} %copy.18, s32[16]{0:T(128)S(1)} %bitcast.41), kind=kOutput, calls=%fused_computation | convolution fusion | flops 100663552 | bytes 4194368 | tf_op jit(solution)/shard_map/ns,sif->nif/dot_general | solution.py:50
  99.1 2.6 %copy.12 = f32[16,128,256]{2,1,0:T(8,128)} copy(f32[16,128,256]{2,0,1:T(8,128)S(1)} %fusion) | data formatting | bytes 4194304 | tf_op jit(solution)/shard_map/ns,sif->nif/dot_general | solution.py:50
  101.6 0.0 copy-start.2
  101.6 0.0 reduce-scatter.2.cloned.1.call-update
  101.6 0.0 all-reduce.8.cloned.1.call-start
  101.7 0.9 copy-done.2
  102.6 1.3 fusion.27
  103.9 0.0 all-reduce.8.cloned.1.call-update
  103.9 0.0 all-reduce.6.cloned.1.call-start
  103.9 38.8 %reduce-scatter.2.cloned.1.call-done = f32[256,256]{1,0:T(8,128)} async-done(((f32[2048,256]{1,0:T(8,128)}), f32[256,256]{1,0:T(8,128)}) %reduce-scatter.2.cloned.1.call-update) | async-done | bytes 262160 | tf_op jit(solution)/shard_map/reduce_scatter | solution.py:49
  142.8 0.0 all-reduce.6.cloned.1.call-update
  142.8 13.2 %psum.31 = f32[256]{0:T(256)} all-reduce(f32[256]{0:T(256)S(1)} %get-tuple-element.4), channel_id=1, replica_groups=mesh['dom'=8,'rep'=4] {'dom'}, use_global_device_ids=true, to_apply=%region_5.0 | all-reduce | flops 256 | bytes 2048 | tf_op jit(solution)/shard_map/psum | solution.py:42
  156.0 43.8 %all-reduce.8.cloned.1.call-done = f32[256,256]{1,0:T(8,128)} async-done(((f32[256,256]{1,0:T(8,128)}), f32[256,256]{1,0:T(8,128)}) %all-reduce.8.cloned.1.call-update) | async-done | bytes 262160 | tf_op jit(solution)/shard_map/psum | solution.py:42
  199.8 37.0 %all-reduce.6.cloned.1.call-done = f32[256,256]{1,0:T(8,128)} async-done(((f32[256,256]{1,0:T(8,128)}), f32[256,256]{1,0:T(8,128)}) %all-reduce.6.cloned.1.call-update) | async-done | bytes 262160 | tf_op jit(solution)/shard_map/psum | solution.py:57
  236.8 1.7 copy.30
  238.5 1.7 copy.31
Async XLA Ops:
  7.2 37.3 %copy-start = (bf16[1,16,128,128]{3,2,1,0:T(8,128)(2,1)S(1)}, bf16[1,16,128,128]{3,2,1,0:T(8,128)(2,1)}, u32[]{:S(2)}) copy-start(bf16[1,16,128,128]{3,2,1,0:T(8,128)(2,1)} %param.8) | copy-start | bytes 1572868
  7.2 33.4 %all-gather.2.cloned.1.call-start = ((), (), s32[]{:S(2)}) async-start(), calls=%async_computation.1 | async-start | bytes 2359296 | tf_op jit(solution)/shard_map/all_gather | solution.py:16
  7.9 79.9 %all-reduce.4.cloned.1.call-start = ((), (), s32[]{:S(2)}) async-start(), calls=%async_computation.2 | async-start | bytes 524288 | tf_op jit(solution)/shard_map/psum | solution.py:29
  48.5 2.3 copy-start.3
  50.8 37.1 %copy-start.1 = (f32[256,256]{1,0:T(8,128)S(1)}, f32[256,256]{1,0:T(8,128)}, u32[]{:S(2)}) copy-start(f32[256,256]{1,0:T(8,128)} %param.11) | copy-start | bytes 786436
  50.8 37.0 %copy-start.5 = (f32[256,256]{1,0:T(8,128)S(1)}, f32[256,256]{1,0:T(8,128)}, u32[]{:S(2)}) copy-start(f32[256,256]{1,0:T(8,128)} %param.13) | copy-start | bytes 786436
  50.8 37.0 %copy-start.6 = (f32[256]{0:T(256)S(1)}, f32[256]{0:T(256)}, u32[]{:S(2)}) copy-start(f32[256]{0:T(256)} %param.12) | copy-start | bytes 3076
  52.4 90.4 %reduce-scatter.2.cloned.1.call-start = ((), (), s32[]{:S(2)}) async-start(), calls=%async_computation.3 | async-start | bytes 2359296 | tf_op jit(solution)/shard_map/reduce_scatter | solution.py:49
  94.3 2.1 copy-start.4
  101.6 0.9 copy-start.2
  101.6 98.2 %all-reduce.8.cloned.1.call-start = ((), (), s32[]{:S(2)}) async-start(), calls=%async_computation.5 | async-start | bytes 524288 | tf_op jit(solution)/shard_map/psum | solution.py:42
  103.9 132.9 %all-reduce.6.cloned.1.call-start = ((), (), s32[]{:S(2)}) async-start(), calls=%async_computation.4 | async-start | bytes 524288 | tf_op jit(solution)/shard_map/psum | solution.py:57
Sparse Core Ops, SparseCore 0:
  9.9 30.5 all-gather.1
  52.5 35.2 all-reduce.3
  101.8 40.9 reduce-scatter.1
  146.2 53.5 all-reduce.7
  202.1 34.6 all-reduce.5
where the time goes:
time: 247 us
  waiting for transfers between devices  188 us (76%)
  matrix products  19.2 us (8%)
  between operations  13.9 us (6%)
  blocking collectives  13.2 us (5%)
  local copies, waits for them, and re-layouts  11.8 us (5%)
    psum x1, waiting for transfers between devices, body(): grad_weight, grad_bias = lax.psum((weight_term, bias_term), 'dom')  43.8 us
    reduce_scatter x1, waiting for transfers between devices, body(): lax.psum_scatter(jnp.einsum('ns,sif->nif', select, returned, precision=hi...  38.8 us
    psum x1, waiting for transfers between devices, body(): grad_features = lax.psum(source_part, 'rep')  37 us
    psum x1, waiting for transfers between devices, body(): aggregated = lax.psum(partial_rows, 'rep')  35.2 us
    all_gather x1, waiting for transfers between devices, body(): shard_piece = lax.all_gather(features, 'dom', axis=0, tiled=True)  32.6 us
    psum x1, blocking collectives, body(): grad_weight, grad_bias = lax.psum((weight_term, bias_term), 'dom')  13.2 us
  transfers between devices with their start and end apart: 5, of which 5 were waited for; matrix products, arithmetic and copies ran while one was open for 1% of the time, Pallas kernels for 0%

commit v1 on v0

--- a/solution.py
+++ b/solution.py
@@ -54,7 +54,7 @@
         scatter_dimension=0,
         tiled=True,
     )
-    grad_features = lax.psum(source_part, "rep")
+    grad_features = jnp.sum(lax.all_gather(source_part, "rep"), axis=0)
     return (activations, grad_features, grad_weight, grad_bias)
 
 

time: 247 us -> 237 us (0.960)
  waiting for transfers between devices: 188 us -> 179 us
  local copies, waits for them, and re-layouts: 11.8 us -> 9.3 us
    psum x1 -> x0, waiting for transfers between devices: 37 us -> none  [body(): grad_features = lax.psum(source_part, 'rep')]
    all_gather x0 -> x1, waiting for transfers between devices: none -> 14.7 us  [body(): grad_features = jnp.sum(lax.all_gather(source_part, 'rep'), axis=0)]
    psum x1, waiting for transfers between devices: 43.8 us -> 54.5 us  [body(): grad_weight, grad_bias = lax.psum((weight_term, bias_term), 'dom')]
    unnamed x16 -> x15, local copies, waits for them, and re-layouts: 4.25 us -> 1.71 us
where the time goes in v1:
time: 237 us
  waiting for transfers between devices  179 us (76%)
  matrix products  19.2 us (8%)
  between operations  13.9 us (6%)
  blocking collectives  13.2 us (6%)
  local copies, waits for them, and re-layouts  9.3 us (4%)
    psum x1, waiting for transfers between devices, body(): grad_weight, grad_bias = lax.psum((weight_term, bias_term), 'dom')  54.5 us
    reduce_scatter x1, waiting for transfers between devices, body(): lax.psum_scatter(jnp.einsum('ns,sif->nif', select, returned, precision=hi...  41.1 us
    psum x1, waiting for transfers between devices, body(): aggregated = lax.psum(partial_rows, 'rep')  35.2 us
    all_gather x1, waiting for transfers between devices, body(): shard_piece = lax.all_gather(features, 'dom', axis=0, tiled=True)  32.6 us
    all_gather x1, waiting for transfers between devices, body(): grad_features = jnp.sum(lax.all_gather(source_part, 'rep'), axis=0)  14.7 us
    psum x1, blocking collectives, body(): grad_weight, grad_bias = lax.psum((weight_term, bias_term), 'dom')  13.2 us
  transfers between devices with their start and end apart: 5, of which 5 were waited for; matrix products, arithmetic and copies ran while one was open for 1% of the time, Pallas kernels for 0%

profile of v1, /device:TPU:0, one launch (start us, length us, event | category | flops | bytes accessed | tf_op | source)
XLA Modules:
  0.0 236.9 jit_solution(10176714849986037155)
XLA Ops:
  7.2 0.0 copy-start
  7.2 0.0 all-gather.4.cloned.1.call-start
  7.2 0.7 all-gather.4.cloned.1.call-update
  7.9 0.0 all-reduce.3.cloned.1.call-start
  8.0 32.6 %all-gather.4.cloned.1.call-done = f32[2048,256]{1,0:T(8,128)} async-done(((f32[256,256]{1,0:T(8,128)}), f32[2048,256]{1,0:T(8,128)}) %all-gather.4.cloned.1.call-update) | async-done | bytes 2097168 | tf_op jit(solution)/shard_map/all_gather | solution.py:16
  40.5 3.9 %fusion.8 = f32[16,128,256]{2,0,1:T(8,128)S(1)} fusion(f32[16,128,256]{2,1,0:T(8,128)} %bitcast.36, s32[16]{0:T(128)} %bitcast.42), kind=kOutput, calls=%fused_computation.8 | convolution fusion | flops 100663552 | bytes 4194368 | tf_op jit(solution)/shard_map/sn,nif->sif/dot_general | solution.py:21
  44.5 0.0 copy-done
  44.5 4.1 %fusion.6 = f32[16,256,128]{2,1,0:T(8,128)} fusion(f32[16,128,256]{2,0,1:T(8,128)S(1)} %fusion.8, bf16[1,16,128,128]{3,2,1,0:T(8,128)(2,1)S(1)} %copy-done), kind=kOutput, calls=%fused_computation.6 | convolution fusion | flops 805306368 | bytes 4718592 | tf_op jit(solution)/shard_map/sij,sjf->sif/dot_general | solution.py:22
  48.5 0.0 copy-start.3
  48.5 2.2 copy.15
  50.8 0.0 copy-start.1
  50.8 0.0 copy-start.5
  50.8 0.0 copy-start.6
  50.8 0.0 copy-done.3
  50.8 0.8 fusion.2
  51.6 0.7 copy.11
  52.4 0.0 all-reduce.3.cloned.1.call-update
  52.4 0.2 reduce-scatter.2.cloned.1.call-start
  52.6 35.2 %all-reduce.3.cloned.1.call-done = f32[256,256]{1,0:T(8,128)} async-done(((f32[256,256]{1,0:T(8,128)}), f32[256,256]{1,0:T(8,128)}) %all-reduce.3.cloned.1.call-update) | async-done | bytes 262160 | tf_op jit(solution)/shard_map/psum | solution.py:29
  87.9 0.0 copy-done.1
  87.9 0.0 copy-done.5
  87.9 0.0 copy-done.6
  87.9 2.1 fusion.25
  90.0 0.4 fusion.26
  90.4 1.1 fusion.12
  91.5 2.7 %fusion.4 = f32[16,256,128]{2,1,0:T(8,128)S(1)} fusion(f32[16,128,256]{2,0,1:T(8,128)S(1)} %fusion.12, bf16[1,16,128,128]{3,2,1,0:T(8,128)(2,1)S(1)} %copy-done), kind=kOutput, calls=%fused_computation.4 | convolution fusion | flops 805306368 | bytes 4718592 | tf_op jit(solution)/shard_map/sji,sjf->sif/dot_general | solution.py:45
  94.3 0.0 copy-start.4
  94.3 2.1 copy.18
  96.4 0.0 copy-done.4
  96.4 2.7 %fusion = f32[16,128,256]{2,0,1:T(8,128)S(1)} fusion(f32[16,256,128]{1,0,2:T(8,128)} %copy.18, s32[16]{0:T(128)S(1)} %bitcast.43), kind=kOutput, calls=%fused_computation | convolution fusion | flops 100663552 | bytes 4194368 | tf_op jit(solution)/shard_map/ns,sif->nif/dot_general | solution.py:50
  99.1 2.6 %copy.12 = f32[16,128,256]{2,1,0:T(8,128)} copy(f32[16,128,256]{2,0,1:T(8,128)S(1)} %fusion) | data formatting | bytes 4194304 | tf_op jit(solution)/shard_map/ns,sif->nif/dot_general | solution.py:50
  101.6 0.0 copy-start.2
  101.6 0.0 reduce-scatter.2.cloned.1.call-update
  101.6 0.0 all-gather.6.cloned.1.call-start
  101.7 41.1 %reduce-scatter.2.cloned.1.call-done = f32[256,256]{1,0:T(8,128)} async-done(((f32[2048,256]{1,0:T(8,128)}), f32[256,256]{1,0:T(8,128)}) %reduce-scatter.2.cloned.1.call-update) | async-done | bytes 262160 | tf_op jit(solution)/shard_map/reduce_scatter | solution.py:49
  142.8 0.0 all-gather.6.cloned.1.call-update
  142.8 0.0 all-reduce.5.cloned.1.call-start
  142.8 0.0 copy-done.2
  142.8 1.3 fusion.27
  144.1 0.0 all-reduce.5.cloned.1.call-update
  144.2 13.2 %psum.23 = f32[256]{0:T(256)} all-reduce(f32[256]{0:T(256)S(1)} %get-tuple-element.4), channel_id=1, replica_groups=mesh['dom'=8,'rep'=4] {'dom'}, use_global_device_ids=true, to_apply=%region_5.0 | all-reduce | flops 256 | bytes 2048 | tf_op jit(solution)/shard_map/psum | solution.py:42
  157.4 14.7 %all-gather.6.cloned.1.call-done = f32[1024,256]{1,0:T(8,128)} async-done(((f32[256,256]{1,0:T(8,128)}), f32[1024,256]{1,0:T(8,128)}) %all-gather.6.cloned.1.call-update) | async-done | bytes 1048592 | tf_op jit(solution)/shard_map/all_gather | solution.py:57
  172.1 2.0 reduce_sum.18
  174.2 54.5 %all-reduce.5.cloned.1.call-done = f32[256,256]{1,0:T(8,128)} async-done(((f32[256,256]{1,0:T(8,128)}), f32[256,256]{1,0:T(8,128)}) %all-reduce.5.cloned.1.call-update) | async-done | bytes 262160 | tf_op jit(solution)/shard_map/psum | solution.py:42
  228.7 1.7 copy.29
Async XLA Ops:
  7.2 37.3 %copy-start = (bf16[1,16,128,128]{3,2,1,0:T(8,128)(2,1)S(1)}, bf16[1,16,128,128]{3,2,1,0:T(8,128)(2,1)}, u32[]{:S(2)}) copy-start(bf16[1,16,128,128]{3,2,1,0:T(8,128)(2,1)} %param.8) | copy-start | bytes 1572868
  7.2 33.4 %all-gather.4.cloned.1.call-start = ((), (), s32[]{:S(2)}) async-start(), calls=%async_computation.1 | async-start | bytes 2359296 | tf_op jit(solution)/shard_map/all_gather | solution.py:16
  7.9 79.9 %all-reduce.3.cloned.1.call-start = ((), (), s32[]{:S(2)}) async-start(), calls=%async_computation.2 | async-start | bytes 524288 | tf_op jit(solution)/shard_map/psum | solution.py:29
  48.5 2.3 copy-start.3
  50.8 37.1 %copy-start.1 = (f32[256,256]{1,0:T(8,128)S(1)}, f32[256,256]{1,0:T(8,128)}, u32[]{:S(2)}) copy-start(f32[256,256]{1,0:T(8,128)} %param.11) | copy-start | bytes 786436
  50.8 37.0 %copy-start.5 = (f32[256,256]{1,0:T(8,128)S(1)}, f32[256,256]{1,0:T(8,128)}, u32[]{:S(2)}) copy-start(f32[256,256]{1,0:T(8,128)} %param.13) | copy-start | bytes 786436
  50.8 37.0 %copy-start.6 = (f32[256]{0:T(256)S(1)}, f32[256]{0:T(256)}, u32[]{:S(2)}) copy-start(f32[256]{0:T(256)} %param.12) | copy-start | bytes 3076
  52.4 90.4 %reduce-scatter.2.cloned.1.call-start = ((), (), s32[]{:S(2)}) async-start(), calls=%async_computation.3 | async-start | bytes 2359296 | tf_op jit(solution)/shard_map/reduce_scatter | solution.py:49
  94.3 2.1 copy-start.4
  101.6 41.2 %copy-start.2 = (f32[256,256]{1,0:T(8,128)S(1)}, f32[256,256]{1,0:T(8,128)}, u32[]{:S(2)}) copy-start(f32[256,256]{1,0:T(8,128)} %all-reduce.3.cloned.1.call-done) | copy-start | bytes 786436
  101.6 70.5 %all-gather.6.cloned.1.call-start = ((), (), s32[]{:S(2)}) async-start(), calls=%async_computation.5 | async-start | bytes 1310720 | tf_op jit(solution)/shard_map/all_gather | solution.py:57
  142.8 85.9 %all-reduce.5.cloned.1.call-start = ((), (), s32[]{:S(2)}) async-start(), calls=%async_computation.4 | async-start | bytes 524288 | tf_op jit(solution)/shard_map/psum | solution.py:42
Sparse Core Ops, SparseCore 0:
  9.9 30.5 all-gather.3
  52.5 35.2 all-reduce.2
  101.8 40.9 reduce-scatter.1
  144.2 27.9 all-gather.5
  175.6 53.0 all-reduce.4
